TPU v7x, 512 devices: a whole 4x4x16 slice. The times are simulated.
512 devices in a mesh: rep: 32 (over z, x_lo), gz: 16 (over x_hi, y, core).
Axes of the slice: x: 4 (x_hi: 2, x_lo: 2; x = x_hi * 2 + x_lo), y: 4, z: 16, core: 2. Of those that a mesh axis runs over, the one named last changes fastest.
Arguments:
- lattice_field: float32 [192, 64, 4096], P('rep', 'gz'), may hold values from -4 to 4
- langevin_noise: float32 [2, 192, 64, 4096], P(None, 'rep', 'gz'), may hold values from -5 to 5
- masses: float32 [64, 4096], P('gz'), may hold values from -2 to 2
- counts: int32 [192], replicated, may hold values from 0 to 49, as said below
- dest_slots: int32 [192], replicated, may hold values from 0 to 191, each once
- mode_bins: int32 [64, 64, 33], P('gz'), may hold values from 0 to 15, as said below
Outputs:
- resampled: float32 [192, 64, 4096], P('rep', 'gz')
- propagator: float32 [192, 16], P('rep')
Inputs may be any that keep to these rules, and one draw needn't show every extreme that they name: The counts sum to 192; in each aligned block of 6 replicas (those of one index of rep) at most 3 counts are nonzero, and exactly 3 in some block. `dest_slots`: A permutation of the 192 slots. `mode_bins`: the bin depends only on n_y^2 + n_z^2 + kx^2 with n = min(k, 64 - k), and never falls as that grows; every bin holds at least one mode.
All inputs are finite; a program needn't handle non-finite values.
Results may differ from a plain program's by a relative error of at most 0.00007.
Values sent between devices are 32-bit elements; how exact they have to be, the bound alone decides.
No kernel may reach another device: no remote copies, remote signals or barrier semaphores. Data moves between devices by JAX's collectives and lax.ppermute only.
A program may use at most 64 MiB of HBM per device.

v0:
```python
import jax
import jax.numpy as jnp
from jax import lax
from jax.sharding import PartitionSpec as P

L = 64
SWEEPS = 2
NBINS = 16
step_size = 0.1
quartic = 0.5


def with_halo(block, sides, width):
    for axis, dim in sides:
        count = lax.axis_size(axis)
        forward = [(i, i + 1) for i in range(count - 1)]
        forward.append((count - 1, 0))
        backward = [(target, source) for source, target in forward]
        low = lax.ppermute(
            lax.slice_in_dim(block, block.shape[dim] - width, None, axis=dim), axis, forward
        )
        high = lax.ppermute(lax.slice_in_dim(block, 0, width, axis=dim), axis, backward)
        block = jnp.concatenate([low, block, high], axis=dim)
    return block


def in_plane(center):
    grid = center.reshape(center.shape[0], center.shape[1], L, L)
    across = jnp.roll(grid, 1, axis=3) + jnp.roll(grid, -1, axis=3)
    return jnp.roll(center, L, axis=2) + jnp.roll(center, -L, axis=2) + across.reshape(center.shape)


def update(center, below, above, site_masses, noise_now):
    beside = below + above + in_plane(center)
    drift = 6.0 * center - beside + site_masses[None] * center + quartic * center * center * center
    return center - step_size * drift + jnp.sqrt(2.0 * step_size) * noise_now


def angle_tables(rows, columns):
    product = jnp.arange(rows)[:, None] * jnp.arange(columns)[None, :] % L
    theta = 2.0 * jnp.pi / L * product.astype(jnp.float32)
    return (jnp.cos(theta), jnp.sin(theta))


def make_weights(mode_bins):
    half = L // 2 + 1
    ordered = jnp.transpose(mode_bins, (1, 0, 2))
    wave_x = jnp.arange(half)
    weight_x = jnp.where((wave_x == 0) | (wave_x == L // 2), 1.0, 2.0).astype(jnp.float32)
    onehot = (ordered[..., None] == jnp.arange(NBINS)[None, None, None, :]).astype(jnp.float32)
    return (onehot * weight_x[None, None, :, None]).reshape(-1, NBINS)


def transform(slabs, weights):
    half = L // 2 + 1
    exact = lax.Precision.HIGHEST
    cos_half, sin_half = angle_tables(L, half)
    cos_full, sin_full = angle_tables(L, L)
    along_x = jnp.concatenate([cos_half, -sin_half], axis=1)
    count, depth = (slabs.shape[0], slabs.shape[1])
    grid = slabs.reshape(count, depth, L, L)
    first = jnp.einsum("nzyx,xk->nzyk", grid, along_x, precision=exact)
    real_x, imag_x = (first[..., :half], first[..., half:])
    real_y = jnp.einsum("qy,nzyk->nzqk", cos_full, real_x, precision=exact) + jnp.einsum(
        "qy,nzyk->nzqk", sin_full, imag_x, precision=exact
    )
    imag_y = jnp.einsum("qy,nzyk->nzqk", cos_full, imag_x, precision=exact) - jnp.einsum(
        "qy,nzyk->nzqk", sin_full, real_x, precision=exact
    )
    merged = jnp.concatenate([real_y, imag_y], axis=3).reshape(count, depth, L * 2 * half)
    block = lax.all_to_all(merged, "gz", split_axis=2, concat_axis=1, tiled=True)
    items = block.shape[0]
    pencil = block.reshape(items, L, -1, 2 * half)
    real_p = pencil[..., :half]
    imag_p = pencil[..., half:]
    real_z = jnp.einsum("pz,mzqk->mpqk", cos_full, real_p, precision=exact) + jnp.einsum(
        "pz,mzqk->mpqk", sin_full, imag_p, precision=exact
    )
    imag_z = jnp.einsum("pz,mzqk->mpqk", cos_full, imag_p, precision=exact) - jnp.einsum(
        "pz,mzqk->mpqk", sin_full, real_p, precision=exact
    )
    power = real_z * real_z + imag_z * imag_z
    binned = jnp.dot(power.reshape(items, -1), weights, precision=exact)
    binned_total, weight_total = lax.psum((binned, jnp.sum(weights, axis=0)), "gz")
    return binned_total / (float(L**3) * weight_total)


def local(lattice_field, langevin_noise, masses, counts, dest_slots, mode_bins):
    local_count = lattice_field.shape[0]
    weights = make_weights(mode_bins)
    swept = lattice_field
    for turn in range(SWEEPS):
        padded = with_halo(swept, (("gz", 1),), 1)
        swept = update(padded[:, 1:-1], padded[:, :-2], padded[:, 2:], masses, langevin_noise[turn])
    base = lax.axis_index("rep") * local_count
    ends = jnp.cumsum(counts)
    position = jnp.argsort(dest_slots)
    mine_position = lax.dynamic_slice_in_dim(position, base, local_count)
    mine_source = jnp.sum((ends[None, :] <= mine_position[:, None]).astype(jnp.int32), axis=1)
    empty = jnp.zeros_like(swept)
    piece = lax.all_gather(swept, "rep", axis=0, tiled=True)
    found = (mine_source >= 0) & (mine_source < piece.shape[0])
    chosen = jnp.take(piece, jnp.clip(mine_source, 0, piece.shape[0] - 1), axis=0)
    resampled = jnp.where(found[:, None, None], chosen, empty)
    propagator = transform(resampled, weights)
    return (resampled, propagator)


def solution(mesh):
    in_specs = (
        P("rep", "gz", None),
        P(None, "rep", "gz", None),
        P("gz", None),
        P(),
        P(),
        P("gz", None, None),
    )
    out_specs = (P("rep", "gz", None), P("rep", None))
    return jax.shard_map(local, mesh=mesh, in_specs=in_specs, out_specs=out_specs, check_vma=False)
```

profile of v0, /device:TPU:38, one launch (start us, length us, event | category | flops | bytes accessed | tf_op | source)
XLA Modules:
  0.0 452.3 jit_solution(2166895266252879648)
XLA Ops:
  7.2 1.3 fusion.124
  8.5 1.9 collective-permute-start
  10.4 7.3 %collective-permute-start.1 = (f32[6,1,4096]{2,1,0:T(1,128)S(1)}, f32[6,1,4096]{2,1,0:T(1,128)S(1)}, u32[]{:S(2)}, u32[]{:S(2)}) collective-permute-start(f32[6,1,4096]{2,1,0:T(1,128)S(1)} %get-tuple-element.27), channel_id=1, source_target_pairs={{1,0},{2,1},{3,2},{4,3},{5,4},{6,5},{7,6},{8,7},{9,8},{10,9},{11,1... | collective-permute-start | bytes 294920 | tf_op jit(solution)/shard_map/ppermute | solution.py:22
  17.7 1.4 reshape.93
  19.7 0.7 copy-done
  20.7 0.7 fusion.123
  21.3 0.5 maximum_add_fusion
  21.8 0.3 add.129
  22.2 0.6 copy-done.4
  23.0 1.8 fusion.23
  24.7 0.4 reshape.94
  26.0 0.8 fusion.121
  26.9 1.9 collective-permute-start.2
  28.8 7.4 %collective-permute-start.3 = (f32[6,1,4096]{2,1,0:T(1,128)}, f32[6,1,4096]{2,1,0:T(1,128)S(1)}, u32[]{:S(2)}, u32[]{:S(2)}) collective-permute-start(f32[6,1,4096]{2,1,0:T(1,128)} %get-tuple-element.21), channel_id=1, source_target_pairs={{1,0},{2,1},{3,2},{4,3},{5,4},{6,5},{7,6},{8,7},{9,8},{10,9},{11,1... | collective-permute-start | bytes 294920 | tf_op jit(solution)/shard_map/ppermute | solution.py:22
  36.3 0.5 maximum_add_fusion.1
  36.8 0.3 add.138
  37.1 1.5 collective-permute-done.3
  38.6 1.6 fusion.27
  40.4 0.3 reduce-window.9
  41.3 3.2 sort.17
  45.3 281.6 %all-gather.2.cloned.1.call-done = f32[192,4,4096]{2,1,0:T(4,128)} async-done(((f32[6,4,4096]{2,1,0:T(4,128)}), f32[192,4,4096]{2,1,0:T(4,128)}) %all-gather.2.cloned.1.call-update) | async-done | bytes 12582928 | tf_op jit(solution)/shard_map/all_gather | solution.py:101
  326.9 5.4 %gather_fusion = f32[6,4,4096]{2,1,0:T(4,128)S(1)} fusion(f32[192,4,4096]{2,1,0:T(4,128)} %all-gather.2.cloned.1.call-done, s32[1024]{0:T(1024)S(1)} %pad_clamp_fusion), kind=kCustom, calls=%fused_computation | custom fusion | bytes 786456 | tf_op jit(solution)/shard_map/jit(_take)/gather | solution.py:103
  332.3 0.4 gather.7
  332.7 0.8 fusion.7
  333.5 1.4 fusion.14
  335.0 1.6 fusion.10
  336.6 1.6 fusion.5
  338.2 1.4 fusion.4
  339.7 9.3 %copy.65 = f32[6,4,64,66]{0,1,3,2:T(4,128)} copy(f32[6,4,64,66]{2,3,1,0:T(8,128)S(1)} %pad_maximum_fusion) | data formatting | bytes 811008 | tf_op jit(solution)/shard_map/reshape | solution.py:70
  349.0 12.4 %reshape.110 = f32[16,1,6336]{2,1,0:T(1,128)} reshape(f32[4224,4,6]{2,1,0:T(4,128)} %bitcast.64) | data formatting | bytes 811008
  361.4 7.3 %all-to-all-start = ((f32[16,1,6336]{2,1,0:T(1,128)}), f32[16,1,6336]{2,1,0:T(1,128)S(1)}, u32[]{:S(2)}, u32[]{:S(2)}) async-start(f32[16,1,6336]{2,1,0:T(1,128)} %reshape.110), calls=%async_computation | async-start | bytes 819200 | tf_op jit(solution)/shard_map/all_to_all | solution.py:71
  368.7 0.9 select_select_fusion
  369.6 7.4 %all-to-all-done = f32[16,1,6336]{2,1,0:T(1,128)S(1)} async-done(((f32[16,1,6336]{2,1,0:T(1,128)}), f32[16,1,6336]{2,1,0:T(1,128)S(1)}, u32[]{:S(2)}, u32[]{:S(2)}) %all-to-all-start) | async-done | bytes 405536 | tf_op jit(solution)/shard_map/all_to_all | solution.py:71
  376.9 0.5 broadcast.218
  377.5 1.6 reduce.2
  379.1 15.2 %reshape.111 = f32[4224,4,6]{2,1,0:T(4,128)} reshape(f32[16,6336]{1,0:T(8,128)S(1)} %reduce.2) | data formatting | bytes 811008
  394.3 7.6 %copy.51 = f32[6,4,16,264]{3,1,2,0:T(4,128)S(1)} copy(f32[6,4,16,264]{0,1,3,2:T(4,128)} %bitcast.65) | data formatting | bytes 811008 | tf_op jit(solution)/shard_map/all_to_all | solution.py:71
  401.9 0.6 reshape.96
  402.5 0.5 fusion.114
  402.9 0.3 copy.67
  403.3 0.7 fusion.56
  404.0 0.3 copy.68
  404.3 0.7 fusion.54
  405.0 0.7 fusion.3
  405.7 0.7 fusion.2
  406.4 1.6 convolution_bitcast_fusion
  407.9 36.9 %all-reduce.1 = (f32[6,16]{1,0:T(8,128)S(1)}, f32[16]{0:T(128)S(1)}) all-reduce(f32[6,16]{1,0:T(8,128)S(1)} %convolution_bitcast_fusion, f32[16]{0:T(128)S(1)} %select_reduce_fusion), channel_id=1, replica_groups=mesh['rep'=32,'gz'=16] {'gz'}, use_global_device_ids=true, to_apply=%region_4.5 | all-reduce | flops 112 | bytes 896 | tf_op jit(solution)/shard_map/psum | solution.py:84
  444.9 0.6 broadcast_divide_fusion
  (47 shorter events, 3.7 us)
Async XLA Ops:
  7.2 319.8 %all-gather.2.cloned.1.call-start = ((), (), s32[]{:S(2)}) async-start(), calls=%async_computation.1 | async-start | bytes 12976128 | tf_op jit(solution)/shard_map/all_gather | solution.py:101
  8.5 13.6 %collective-permute-start = (f32[6,1,4096]{2,1,0:T(1,128)S(1)}, f32[6,1,4096]{2,1,0:T(1,128)S(1)}, u32[]{:S(2)}, u32[]{:S(2)}) collective-permute-start(f32[6,1,4096]{2,1,0:T(1,128)S(1)} %get-tuple-element.26), channel_id=1, source_target_pairs={{0,1},{1,2},{2,3},{3,4},{4,5},{5,6},{6,7},{7,8},{8,9},{9,10},{10,1... | collective-permute-start | bytes 294920 | tf_op jit(solution)/shard_map/ppermute | solution.py:19
  10.4 11.7 %collective-permute-start.1 = (f32[6,1,4096]{2,1,0:T(1,128)S(1)}, f32[6,1,4096]{2,1,0:T(1,128)S(1)}, u32[]{:S(2)}, u32[]{:S(2)}) collective-permute-start(f32[6,1,4096]{2,1,0:T(1,128)S(1)} %get-tuple-element.27), channel_id=1, source_target_pairs={{1,0},{2,1},{3,2},{4,3},{5,4},{6,5},{7,6},{8,7},{9,8},{10,9},{11,1... | collective-permute-start | bytes 294920 | tf_op jit(solution)/shard_map/ppermute | solution.py:22
  19.4 1.0 copy-start
  21.8 1.1 copy-start.1
  22.2 0.6 copy-start.4
  22.2 0.7 copy-start.5
  26.9 10.2 %collective-permute-start.2 = (f32[6,1,4096]{2,1,0:T(1,128)}, f32[6,1,4096]{2,1,0:T(1,128)S(1)}, u32[]{:S(2)}, u32[]{:S(2)}) collective-permute-start(f32[6,1,4096]{2,1,0:T(1,128)} %get-tuple-element.20), channel_id=1, source_target_pairs={{0,1},{1,2},{2,3},{3,4},{4,5},{5,6},{6,7},{7,8},{8,9},{9,10},{10,1... | collective-permute-start | bytes 294920 | tf_op jit(solution)/shard_map/ppermute | solution.py:19
  28.8 9.8 %collective-permute-start.3 = (f32[6,1,4096]{2,1,0:T(1,128)}, f32[6,1,4096]{2,1,0:T(1,128)S(1)}, u32[]{:S(2)}, u32[]{:S(2)}) collective-permute-start(f32[6,1,4096]{2,1,0:T(1,128)} %get-tuple-element.21), channel_id=1, source_target_pairs={{1,0},{2,1},{3,2},{4,3},{5,4},{6,5},{7,6},{8,7},{9,8},{10,9},{11,1... | collective-permute-start | bytes 294920 | tf_op jit(solution)/shard_map/ppermute | solution.py:22
  36.8 1.9 copy-start.3
  38.6 1.6 copy-start.2
  38.6 1.8 copy-start.6
  40.2 1.1 copy-start.7
  361.4 15.5 %all-to-all-start = ((f32[16,1,6336]{2,1,0:T(1,128)}), f32[16,1,6336]{2,1,0:T(1,128)S(1)}, u32[]{:S(2)}, u32[]{:S(2)}) async-start(f32[16,1,6336]{2,1,0:T(1,128)} %reshape.110), calls=%async_computation | async-start | bytes 819200 | tf_op jit(solution)/shard_map/all_to_all | solution.py:71
Sparse Core Ops, SparseCore 0:
  40.3 286.5 all-gather.1
where the time goes:
time: 453 us; the launch traced here: 452 us
  waiting for transfers between devices  290 us (64%)
  local copies, waits for them, and re-layouts  61.9 us (14%)
  blocking collectives  36.9 us (8%)
  starting transfers between devices  25.8 us (6%)
  between operations  14.4 us (3%)
  other arithmetic  11.6 us (3%)
  matrix products  11.2 us (2%)
    all_gather x1, waiting for transfers between devices, local(): piece = lax.all_gather(swept, 'rep', axis=0, tiled=True)  282 us
    psum x1, blocking collectives, transform(): lax.psum((binned, jnp.sum(weights, axis=0)), 'gz')  36.9 us
    unnamed x20, local copies, waits for them, and re-layouts  29.8 us
    ppermute x2, starting transfers between devices, with_halo(): lax.ppermute(lax.slice_in_dim(block, 0, width, axis=dim), axis, backward)  14.7 us
    reshape x1, local copies, waits for them, and re-layouts, transform(): jnp.concatenate([real_y, imag_y], axis=3)  9.27 us
  transfers between devices with their start and end apart: 6, of which 3 were waited for; matrix products, arithmetic and copies ran while one was open for 2% of the time, Pallas kernels for 0%

commit v1 on v0

--- a/solution.py
+++ b/solution.py
@@ -68,7 +68,9 @@
         "qy,nzyk->nzqk", sin_full, real_x, precision=exact
     )
     merged = jnp.concatenate([real_y, imag_y], axis=3).reshape(count, depth, L * 2 * half)
-    block = lax.all_to_all(merged, "gz", split_axis=2, concat_axis=1, tiled=True)
+    cells = jnp.split(merged, lax.axis_size("gz"), axis=2)
+    received = lax.all_to_all(jnp.stack(cells), "gz", 0, 0)
+    block = jnp.concatenate(received, axis=1)
     items = block.shape[0]
     pencil = block.reshape(items, L, -1, 2 * half)
     real_p = pencil[..., :half]

time: 453 us -> 420 us (0.927)
  local copies, waits for them, and re-layouts: 61.9 us -> 28.9 us
    unnamed x20 -> x33, local copies, waits for them, and re-layouts: 29.8 us -> 12.5 us
    reshape x1, local copies, waits for them, and re-layouts: 9.27 us -> 0.59 us  [transform(): jnp.concatenate([real_y, imag_y], axis=3)]
    all_to_all x2 -> x0, local copies, waits for them, and re-layouts: 8.1 us -> none  [transform(): lax.all_to_all(merged, 'gz', split_axis=2, concat_axis=1, tiled=True)]
where the time goes in v1:
time: 420 us
  waiting for transfers between devices  292 us (70%)
  blocking collectives  36.9 us (9%)
  local copies, waits for them, and re-layouts  28.9 us (7%)
  starting transfers between devices  25.8 us (6%)
  between operations  14.4 us (3%)
  matrix products  11.2 us (3%)
  other arithmetic  10 us (2%)
    all_gather x1, waiting for transfers between devices, local(): piece = lax.all_gather(swept, 'rep', axis=0, tiled=True)  282 us
    psum x1, blocking collectives, transform(): lax.psum((binned, jnp.sum(weights, axis=0)), 'gz')  36.9 us
    ppermute x2, starting transfers between devices, with_halo(): lax.ppermute(lax.slice_in_dim(block, 0, width, axis=dim), axis, backward)  14.7 us
    unnamed x33, local copies, waits for them, and re-layouts  12.5 us
    all_to_all x1, waiting for transfers between devices, transform(): received = lax.all_to_all(jnp.stack(cells), 'gz', 0, 0)  9.29 us
  transfers between devices with their start and end apart: 6, of which 3 were waited for; matrix products, arithmetic and copies ran while one was open for 2% of the time, Pallas kernels for 0%

profile of v1, /device:TPU:38, one launch (start us, length us, event | category | flops | bytes accessed | tf_op | source)
XLA Modules:
  0.0 419.7 jit_solution(14231684890054128430)
XLA Ops:
  7.2 1.3 fusion.140
  8.5 1.9 collective-permute-start
  10.4 7.3 %collective-permute-start.1 = (f32[6,1,4096]{2,1,0:T(1,128)S(1)}, f32[6,1,4096]{2,1,0:T(1,128)S(1)}, u32[]{:S(2)}, u32[]{:S(2)}) collective-permute-start(f32[6,1,4096]{2,1,0:T(1,128)S(1)} %get-tuple-element.27), channel_id=1, source_target_pairs={{1,0},{2,1},{3,2},{4,3},{5,4},{6,5},{7,6},{8,7},{9,8},{10,9},{11,1... | collective-permute-start | bytes 294920 | tf_op jit(solution)/shard_map/ppermute | solution.py:22
  17.7 1.4 reshape.92
  19.7 0.7 copy-done
  20.7 0.7 fusion.139
  22.2 0.6 copy-done.4
  23.0 1.8 fusion.23
  26.0 0.8 fusion.137
  26.9 1.9 collective-permute-start.2
  28.8 7.4 %collective-permute-start.3 = (f32[6,1,4096]{2,1,0:T(1,128)}, f32[6,1,4096]{2,1,0:T(1,128)S(1)}, u32[]{:S(2)}, u32[]{:S(2)}) collective-permute-start(f32[6,1,4096]{2,1,0:T(1,128)} %get-tuple-element.21), channel_id=1, source_target_pairs={{1,0},{2,1},{3,2},{4,3},{5,4},{6,5},{7,6},{8,7},{9,8},{10,9},{11,1... | collective-permute-start | bytes 294920 | tf_op jit(solution)/shard_map/ppermute | solution.py:22
  37.1 1.5 collective-permute-done.3
  38.6 1.6 fusion.27
  41.3 3.2 sort.17
  45.3 281.6 %all-gather.2.cloned.1.call-done = f32[192,4,4096]{2,1,0:T(4,128)} async-done(((f32[6,4,4096]{2,1,0:T(4,128)}), f32[192,4,4096]{2,1,0:T(4,128)}) %all-gather.2.cloned.1.call-update) | async-done | bytes 12582928 | tf_op jit(solution)/shard_map/all_gather | solution.py:103
  326.9 5.4 %gather_fusion = f32[6,4,4096]{2,1,0:T(4,128)S(1)} fusion(f32[192,4,4096]{2,1,0:T(4,128)} %all-gather.2.cloned.1.call-done, s32[1024]{0:T(1024)S(1)} %pad_clamp_fusion), kind=kCustom, calls=%fused_computation | custom fusion | bytes 786456 | tf_op jit(solution)/shard_map/jit(_take)/gather | solution.py:105
  332.7 0.8 fusion.7
  333.6 1.4 fusion.14
  335.0 1.6 fusion.10
  336.6 1.6 fusion.5
  338.2 1.4 fusion.4
  340.1 0.6 reshape.94
  340.7 0.6 fusion.57
  341.3 0.7 fusion.56
  342.0 0.7 fusion.55
  342.7 0.7 fusion.54
  343.4 0.7 fusion.53
  344.1 0.7 fusion.52
  344.8 0.7 fusion.51
  345.5 0.7 fusion.50
  346.1 0.7 fusion.49
  346.8 0.7 fusion.48
  347.5 0.7 fusion.47
  348.2 0.7 fusion.46
  348.9 0.7 fusion.45
  349.6 0.7 fusion.44
  350.3 0.7 fusion.43
  351.0 0.7 fusion.42
  351.7 7.3 %all-to-all-start = ((f32[16,6,4,264]{3,2,1,0:T(4,128)}), f32[16,6,4,264]{3,2,1,0:T(4,128)S(1)}, u32[]{:S(2)}, u32[]{:S(2)}) async-start(f32[16,6,4,264]{3,2,1,0:T(4,128)} %fusion.42), calls=%async_computation | async-start | bytes 1179648 | tf_op jit(solution)/shard_map/all_to_all | solution.py:72
  359.0 0.9 select_select_fusion
  359.9 9.3 %all-to-all-done = f32[16,6,4,264]{3,2,1,0:T(4,128)S(1)} async-done(((f32[16,6,4,264]{3,2,1,0:T(4,128)}), f32[16,6,4,264]{3,2,1,0:T(4,128)S(1)}, u32[]{:S(2)}, u32[]{:S(2)}) %all-to-all-start) | async-done | bytes 405536 | tf_op jit(solution)/shard_map/all_to_all | solution.py:72
  370.6 0.7 fusion.72
  371.6 0.7 fusion.70
  372.3 0.7 fusion.3
  373.0 0.7 fusion.2
  373.7 1.6 convolution_bitcast_fusion
  375.3 36.9 %all-reduce.1 = (f32[6,16]{1,0:T(8,128)S(1)}, f32[16]{0:T(128)S(1)}) all-reduce(f32[6,16]{1,0:T(8,128)S(1)} %convolution_bitcast_fusion, f32[16]{0:T(128)S(1)} %select_reduce_fusion), channel_id=1, replica_groups=mesh['rep'=32,'gz'=16] {'gz'}, use_global_device_ids=true, to_apply=%region_4.5 | all-reduce | flops 112 | bytes 896 | tf_op jit(solution)/shard_map/psum | solution.py:86
  412.2 0.6 broadcast_divide_fusion
  (60 shorter events, 8.4 us)
Async XLA Ops:
  7.2 319.8 %all-gather.2.cloned.1.call-start = ((), (), s32[]{:S(2)}) async-start(), calls=%async_computation.1 | async-start | bytes 12976128 | tf_op jit(solution)/shard_map/all_gather | solution.py:103
  8.5 13.6 %collective-permute-start = (f32[6,1,4096]{2,1,0:T(1,128)S(1)}, f32[6,1,4096]{2,1,0:T(1,128)S(1)}, u32[]{:S(2)}, u32[]{:S(2)}) collective-permute-start(f32[6,1,4096]{2,1,0:T(1,128)S(1)} %get-tuple-element.26), channel_id=1, source_target_pairs={{0,1},{1,2},{2,3},{3,4},{4,5},{5,6},{6,7},{7,8},{8,9},{9,10},{10,1... | collective-permute-start | bytes 294920 | tf_op jit(solution)/shard_map/ppermute | solution.py:19
  10.4 11.7 %collective-permute-start.1 = (f32[6,1,4096]{2,1,0:T(1,128)S(1)}, f32[6,1,4096]{2,1,0:T(1,128)S(1)}, u32[]{:S(2)}, u32[]{:S(2)}) collective-permute-start(f32[6,1,4096]{2,1,0:T(1,128)S(1)} %get-tuple-element.27), channel_id=1, source_target_pairs={{1,0},{2,1},{3,2},{4,3},{5,4},{6,5},{7,6},{8,7},{9,8},{10,9},{11,1... | collective-permute-start | bytes 294920 | tf_op jit(solution)/shard_map/ppermute | solution.py:22
  19.4 1.0 copy-start
  21.8 1.1 copy-start.1
  22.2 0.6 copy-start.4
  22.2 0.7 copy-start.5
  26.9 10.2 %collective-permute-start.2 = (f32[6,1,4096]{2,1,0:T(1,128)}, f32[6,1,4096]{2,1,0:T(1,128)S(1)}, u32[]{:S(2)}, u32[]{:S(2)}) collective-permute-start(f32[6,1,4096]{2,1,0:T(1,128)} %get-tuple-element.20), channel_id=1, source_target_pairs={{0,1},{1,2},{2,3},{3,4},{4,5},{5,6},{6,7},{7,8},{8,9},{9,10},{10,1... | collective-permute-start | bytes 294920 | tf_op jit(solution)/shard_map/ppermute | solution.py:19
  28.8 9.8 %collective-permute-start.3 = (f32[6,1,4096]{2,1,0:T(1,128)}, f32[6,1,4096]{2,1,0:T(1,128)S(1)}, u32[]{:S(2)}, u32[]{:S(2)}) collective-permute-start(f32[6,1,4096]{2,1,0:T(1,128)} %get-tuple-element.21), channel_id=1, source_target_pairs={{1,0},{2,1},{3,2},{4,3},{5,4},{6,5},{7,6},{8,7},{9,8},{10,9},{11,1... | collective-permute-start | bytes 294920 | tf_op jit(solution)/shard_map/ppermute | solution.py:22
  36.8 1.9 copy-start.3
  38.6 1.6 copy-start.2
  38.6 1.8 copy-start.6
  40.2 1.1 copy-start.7
  351.7 17.5 %all-to-all-start = ((f32[16,6,4,264]{3,2,1,0:T(4,128)}), f32[16,6,4,264]{3,2,1,0:T(4,128)S(1)}, u32[]{:S(2)}, u32[]{:S(2)}) async-start(f32[16,6,4,264]{3,2,1,0:T(4,128)} %fusion.42), calls=%async_computation | async-start | bytes 1179648 | tf_op jit(solution)/shard_map/all_to_all | solution.py:72
Sparse Core Ops, SparseCore 0:
  40.3 286.5 all-gather.1
